TPU v7x, 512 devices: a whole 4x4x16 slice. The times are simulated.
512 devices in a mesh: blk: 64 (over z, y_lo, core), rows: 8 (over y_hi, x).
Axes of the slice: x: 4, y: 4 (y_hi: 2, y_lo: 2; y = y_hi * 2 + y_lo), z: 16, core: 2. Of those that a mesh axis runs over, the one named last changes fastest.
Arguments:
- blocks: bfloat16 [64, 8, 3, 64, 4096], P('blk', 'rows'), may hold values from -6 to 6
- block_row: int32 [64, 8, 3], P('blk', 'rows'), may hold values from 0 to 7
- block_col: int32 [64, 8, 3], P('blk', 'rows'), may hold values from 0 to 63
- block_ctx: int32 [64, 8, 3], P('blk', 'rows'), may hold values from 0 to 1
- live_blocks: int32 [64, 8], P('blk', 'rows'), may hold values from 1 to 3, as said below
- user_factor: float32 [32768, 256], P(('blk', 'rows')), may hold values from -2.5 to 2.5
- item_factor: float32 [4096, 256], P('blk'), may hold values from -2.5 to 2.5
- context_factor: float32 [128, 256], replicated, may hold values from -2.5 to 2.5
Outputs:
- new_users: float32 [32768, 256], P(('blk', 'rows'))
- new_items: float32 [4096, 256], P('blk')
- context_grad: float32 [128, 256], replicated
Inputs may be any that keep to these rules, and one draw needn't show every extreme that they name: `live_blocks`: every device has at least one used slot; in every draw some device uses all 3 slots.
All inputs are finite; a program needn't handle non-finite values.
Results may differ from a plain program's by a relative error of at most 0.0089.
The roundings to bfloat16 on the way count: a program that leaves them out, or rounds other values in their place, can miss the bound.
Values may be sent and summed in bfloat16 or wider, within the bound.
A program may use at most 64 MiB of HBM per device.

v0:
```python
import math
import jax
import jax.numpy as jnp
from jax import lax
from jax.sharding import PartitionSpec as P

ITERS = 2


def block_terms(block_x, user_rows, item_rows, context_rows, with_context):
    block_edge = user_rows.shape[0]
    factor_rank = user_rows.shape[1]
    user_wide = user_rows.astype(jnp.float32)
    item_wide = item_rows.astype(jnp.float32)
    context_wide = context_rows.astype(jnp.float32)
    pair_vw = (
        (item_wide[:, None, :] * context_wide[None, :, :])
        .astype(jnp.bfloat16)
        .reshape(block_edge * block_edge, factor_rank)
    )
    model_block = lax.dot_general(
        user_rows, pair_vw, (((1,), (1,)), ((), ())), preferred_element_type=jnp.float32
    )
    residual = (model_block - block_x.astype(jnp.float32)).astype(jnp.bfloat16)
    user_term = jnp.dot(residual, pair_vw, preferred_element_type=jnp.float32)
    pair_uw = (
        (user_wide[:, None, :] * context_wide[None, :, :])
        .astype(jnp.bfloat16)
        .reshape(block_edge * block_edge, factor_rank)
    )
    resid_items = (
        residual.reshape(block_edge, block_edge, block_edge)
        .transpose(1, 0, 2)
        .reshape(block_edge, block_edge * block_edge)
    )
    item_term = jnp.dot(resid_items, pair_uw, preferred_element_type=jnp.float32)
    if with_context:
        pair_uv = (
            (user_wide[:, None, :] * item_wide[None, :, :])
            .astype(jnp.bfloat16)
            .reshape(block_edge * block_edge, factor_rank)
        )
        context_term = lax.dot_general(
            residual.reshape(block_edge * block_edge, block_edge),
            pair_uv,
            (((0,), (0,)), ((), ())),
            preferred_element_type=jnp.float32,
        )
    else:
        context_term = jnp.zeros((block_edge, factor_rank), jnp.float32)
    return (user_term, item_term, context_term)


def add_rows(target, start_row, term):
    current = lax.dynamic_slice_in_dim(target, start_row, term.shape[0], 0)
    return lax.dynamic_update_slice_in_dim(target, current + term, start_row, 0)


def local(
    blocks, block_row, block_col, block_ctx, live_blocks, user_factor, item_factor, context_factor
):
    block_edge = blocks.shape[3]
    factor_rank = user_factor.shape[1]
    slot_count = blocks.shape[2]
    slot_blocks = blocks[0, 0]
    rows_of = block_row[0, 0]
    items_of = block_col[0, 0]
    contexts_of = block_ctx[0, 0]
    live_count = live_blocks[0, 0]
    row_groups = lax.axis_size("rows")
    blk_count = lax.axis_size("blk")
    user_step = 6.4 / (block_edge * block_edge)
    item_step = 16.0 / (block_edge * block_edge * row_groups)
    grad_scale = 8.0 / (block_edge * math.sqrt(blk_count * row_groups))
    context_bf = context_factor.astype(jnp.bfloat16)
    context_grad = jnp.zeros(context_factor.shape, jnp.float32)
    for step_index in range(ITERS):
        is_last = step_index == ITERS - 1
        group_users = lax.all_gather(user_factor.astype(jnp.bfloat16), "rows", axis=0, tiled=True)
        all_items = lax.all_gather(item_factor.astype(jnp.bfloat16), "blk", axis=0, tiled=True)

        def visit_block(slot_index, carried):
            user_acc, item_acc, ctx_acc, item_tiles = carried
            block_x = lax.dynamic_index_in_dim(slot_blocks, slot_index, 0, keepdims=False)
            row_at = rows_of[slot_index] * block_edge
            item_at = items_of[slot_index] * block_edge
            ctx_at = contexts_of[slot_index] * block_edge
            user_rows = lax.dynamic_slice_in_dim(group_users, row_at, block_edge, 0)
            item_rows = lax.dynamic_slice_in_dim(all_items, item_at, block_edge, 0)
            context_rows = lax.dynamic_slice_in_dim(context_bf, ctx_at, block_edge, 0)
            user_term, item_term, context_term = block_terms(
                block_x, user_rows, item_rows, context_rows, is_last
            )
            user_acc = add_rows(user_acc, row_at, user_term)
            item_acc = add_rows(item_acc, item_at, item_term)
            item_tiles = lax.dynamic_update_index_in_dim(item_tiles, item_term, slot_index, 0)
            if is_last:
                ctx_acc = add_rows(ctx_acc, ctx_at, context_term)
            return (user_acc, item_acc, ctx_acc, item_tiles)

        start_acc = (
            jnp.zeros((row_groups * block_edge, factor_rank), jnp.float32),
            jnp.zeros((blk_count * block_edge, factor_rank), jnp.float32),
            jnp.zeros(context_factor.shape, jnp.float32),
            jnp.zeros((slot_count, block_edge, factor_rank), jnp.float32),
        )
        user_acc, item_acc, ctx_acc, item_tiles = lax.fori_loop(
            0, live_count, visit_block, start_acc
        )
        own_grad = lax.psum_scatter(user_acc, "rows", scatter_dimension=0, tiled=True)
        received = lax.all_to_all(
            item_acc.reshape(blk_count, block_edge, factor_rank),
            "blk",
            split_axis=0,
            concat_axis=0,
            tiled=True,
        )
        item_grad = lax.psum(jnp.sum(received, axis=0), "rows")
        user_factor = user_factor - user_step * own_grad
        item_factor = item_factor - item_step * item_grad
        if is_last:
            context_grad = lax.psum(ctx_acc, ("blk", "rows")) * grad_scale
    return (user_factor, item_factor, context_grad)


def solution(mesh):
    return jax.shard_map(
        local,
        mesh=mesh,
        in_specs=(
            P("blk", "rows", None, None, None),
            P("blk", "rows", None),
            P("blk", "rows", None),
            P("blk", "rows", None),
            P("blk", "rows"),
            P(("blk", "rows"), None),
            P("blk", None),
            P(),
        ),
        out_specs=(P(("blk", "rows"), None), P("blk", None), P()),
        check_vma=False,
    )
```

profile of v0, /device:TPU:32, one launch (start us, length us, event | category | flops | bytes accessed | tf_op | source)
XLA Modules:
  0.0 1452.8 jit_solution(12432927686246199933)
XLA Ops:
  7.2 1.5 convert_element_type.100
  8.7 0.8 convert_element_type.99
  9.6 0.9 convert_element_type.101
  10.5 35.1 %all_gather.12 = bf16[512,256]{1,0:T(8,128)(2,1)S(1)} all-gather(bf16[64,256]{1,0:T(8,128)(2,1)S(1)} %convert_element_type.99), channel_id=1, replica_groups=mesh['blk'=64,'rows'=8] {'rows'}, dimensions={0}, use_global_device_ids=true | all-gather | bytes 294912 | tf_op jit(solution)/shard_map/all_gather | solution.py:79
  45.6 91.5 %all-gather.3.cloned.1.call-done = bf16[4096,256]{1,0:T(8,128)(2,1)} async-done(((bf16[64,256]{1,0:T(8,128)(2,1)}), bf16[4096,256]{1,0:T(8,128)(2,1)}) %all-gather.3.cloned.1.call-update) | async-done | bytes 2097168 | tf_op jit(solution)/shard_map/all_gather | solution.py:80
  137.2 2.2 broadcast.33.clone
  139.4 12.0 while.30
  140.1 0.6 dynamic_slice.119
  141.3 0.6 dynamic_slice.121
  142.6 0.6 dynamic_slice.120
  143.8 0.8 dynamic-slice_convert_fusion.10
  144.6 0.7 multiply_convert_fusion.24
  145.3 1.8 fusion.57
  147.6 1.1 reshape.90
  148.7 2.0 fusion.59
  151.4 219.3 %all_to_all.10 = f32[64,64,256]{2,1,0:T(8,128)} all-to-all(f32[64,64,256]{2,1,0:T(8,128)} %bitcast.101), channel_id=1, replica_groups=mesh['blk'=64,'rows'=8] {'blk'}, dimensions={0} | all-to-all | bytes 8388608 | tf_op jit(solution)/shard_map/all_to_all | solution.py:111
  370.7 3.1 reduce_sum.18
  373.9 0.7 reduce-scatter.3.cloned.1.call-update
  374.6 92.3 %all-reduce.4.cloned.1.call-done = f32[64,256]{1,0:T(8,128)} async-done(((f32[64,256]{1,0:T(8,128)}), f32[64,256]{1,0:T(8,128)}) %all-reduce.4.cloned.1.call-update) | async-done | bytes 65552 | tf_op jit(solution)/shard_map/psum | solution.py:118
  466.9 1.5 fusion.24
  468.4 87.7 %reduce-scatter.3.cloned.1.call-done = f32[64,256]{1,0:T(8,128)} async-done(((f32[512,256]{1,0:T(8,128)}), f32[64,256]{1,0:T(8,128)}) %reduce-scatter.3.cloned.1.call-update) | async-done | bytes 65552 | tf_op jit(solution)/shard_map/reduce_scatter | solution.py:110
  556.1 0.9 fusion.23
  557.0 36.4 %all_gather.14 = bf16[512,256]{1,0:T(8,128)(2,1)} all-gather(bf16[64,256]{1,0:T(8,128)(2,1)S(1)} %fusion.23), channel_id=1, replica_groups=mesh['blk'=64,'rows'=8] {'rows'}, dimensions={0}, use_global_device_ids=true | all-gather | bytes 294912 | tf_op jit(solution)/shard_map/all_gather | solution.py:79
  593.4 86.8 %all-gather.5.cloned.1.call-done = bf16[4096,256]{1,0:T(8,128)(2,1)} async-done(((bf16[64,256]{1,0:T(8,128)(2,1)}), bf16[4096,256]{1,0:T(8,128)(2,1)}) %all-gather.5.cloned.1.call-update) | async-done | bytes 2097168 | tf_op jit(solution)/shard_map/all_gather | solution.py:80
  680.2 2.3 broadcast.33
  682.5 17.4 %while.31 = (s32[]{:T(128)}, f32[512,256]{1,0:T(8,128)S(1)}, f32[4096,256]{1,0:T(8,128)}, f32[128,256]{1,0:T(8,128)S(1)}, s32[]{:T(128)}, /*index=5*/s32[3]{0:T(...) while((s32[]{:T(128)}, f32[512,256]{1,0:T(8,128)S(1)}, ...), condition=%wide.region_6.7_spmd, body=%wide.region_5.6_spmd.sunk | while | flops 544047104 | bytes 16253349 | solution.py:107
  683.1 0.6 dynamic_slice.129
  684.4 0.6 dynamic_slice.131
  685.6 0.6 dynamic_slice.130
  686.9 0.8 dynamic-slice_convert_fusion.13
  687.6 0.8 dynamic-slice_convert_fusion.12
  688.4 1.5 multiply_convert_fusion.26
  689.9 1.8 fusion.67
  692.2 2.1 reshape.92
  694.3 1.8 fusion.70
  696.0 1.1 reshape.91
  697.2 2.0 fusion.69
  699.9 0.8 copy-done
  700.7 41.5 %all-to-all-start.1 = ((f32[64,64,256]{2,1,0:T(8,128)}), f32[64,64,256]{2,1,0:T(8,128)}, u32[]{:S(2)}, u32[]{:S(2)}) async-start(f32[64,64,256]{2,1,0:T(8,128)} %bitcast.100), calls=%async_computation.3 | async-start | bytes 8388608 | tf_op jit(solution)/shard_map/all_to_all | solution.py:111
  742.2 0.5 all-reduce.8.cloned.1.call-update
  742.8 0.5 reduce-scatter.5.cloned.1.call-update
  743.4 516.1 %all-reduce.8.cloned.1.call-done = f32[128,256]{1,0:T(8,128)} async-done(((f32[128,256]{1,0:T(8,128)}), f32[128,256]{1,0:T(8,128)}) %all-reduce.8.cloned.1.call-update) | async-done | bytes 131088 | tf_op jit(solution)/shard_map/psum | solution.py:122
  1259.5 1.6 broadcast_multiply_fusion
  1261.1 3.1 reduce_sum.19
  1264.2 78.9 %reduce-scatter.5.cloned.1.call-done = f32[64,256]{1,0:T(8,128)} async-done(((f32[512,256]{1,0:T(8,128)}), f32[64,256]{1,0:T(8,128)}) %reduce-scatter.5.cloned.1.call-update) | async-done | bytes 65552 | tf_op jit(solution)/shard_map/reduce_scatter | solution.py:110
  1343.1 1.5 multiply_subtract_fusion.1
  1344.6 99.9 %all-reduce.6.cloned.1.call-done = f32[64,256]{1,0:T(8,128)} async-done(((f32[64,256]{1,0:T(8,128)}), f32[64,256]{1,0:T(8,128)}) %all-reduce.6.cloned.1.call-update) | async-done | bytes 65552 | tf_op jit(solution)/shard_map/psum | solution.py:118
  1444.5 1.5 multiply_subtract_fusion
  (39 shorter events, 1.4 us)
Async XLA Ops:
  7.2 129.9 %all-gather.3.cloned.1.call-start = ((), (), s32[]{:S(2)}) async-start(), calls=%async_computation.4 | async-start | bytes 2129920 | tf_op jit(solution)/shard_map/all_gather | solution.py:80
  8.7 458.2 %all-reduce.4.cloned.1.call-start = ((), (), s32[]{:S(2)}) async-start(), calls=%async_computation.6 | async-start | bytes 131072 | tf_op jit(solution)/shard_map/psum | solution.py:118
  137.1 2.3 copy-start.8
  137.1 2.3 copy-start.9
  137.1 2.3 copy-start.10
  151.4 219.3 %copy-start.1 = (f32[512,256]{1,0:T(8,128)}, f32[512,256]{1,0:T(8,128)S(1)}, u32[]{:S(2)}) copy-start(f32[512,256]{1,0:T(8,128)S(1)} %get-tuple-element.185) | copy-start | bytes 1572868
  370.7 96.2 %copy-start.4 = (f32[64,256]{1,0:T(8,128)S(1)}, f32[64,256]{1,0:T(8,128)}, u32[]{:S(2)}) copy-start(f32[64,256]{1,0:T(8,128)} %param.18) | copy-start | bytes 196612
  370.7 185.4 %copy-start.3 = (f32[64,256]{1,0:T(8,128)S(1)}, f32[64,256]{1,0:T(8,128)}, u32[]{:S(2)}) copy-start(f32[64,256]{1,0:T(8,128)} %param.17) | copy-start | bytes 196612
  373.8 182.3 %reduce-scatter.3.cloned.1.call-start = ((), (), s32[]{:S(2)}) async-start(), calls=%async_computation.5 | async-start | bytes 589824 | tf_op jit(solution)/shard_map/reduce_scatter | solution.py:110
  374.6 305.6 %all-gather.5.cloned.1.call-start = ((), (), s32[]{:S(2)}) async-start(), calls=%async_computation.7 | async-start | bytes 2129920 | tf_op jit(solution)/shard_map/all_gather | solution.py:80
  699.8 0.8 copy-start
  699.9 0.8 copy-start.2
  700.7 560.4 %all-to-all-start.1 = ((f32[64,64,256]{2,1,0:T(8,128)}), f32[64,64,256]{2,1,0:T(8,128)}, u32[]{:S(2)}, u32[]{:S(2)}) async-start(f32[64,64,256]{2,1,0:T(8,128)} %bitcast.100), calls=%async_computation.3 | async-start | bytes 8388608 | tf_op jit(solution)/shard_map/all_to_all | solution.py:111
  742.2 517.3 %all-reduce.8.cloned.1.call-start = ((), (), s32[]{:S(2)}) async-start(), calls=%async_computation.10 | async-start | bytes 262144 | tf_op jit(solution)/shard_map/psum | solution.py:122
  742.8 600.4 %reduce-scatter.5.cloned.1.call-start = ((), (), s32[]{:S(2)}) async-start(), calls=%async_computation.8 | async-start | bytes 589824 | tf_op jit(solution)/shard_map/reduce_scatter | solution.py:110
  743.3 701.2 %all-reduce.6.cloned.1.call-start = ((), (), s32[]{:S(2)}) async-start(), calls=%async_computation.9 | async-start | bytes 131072 | tf_op jit(solution)/shard_map/psum | solution.py:118
  1261.1 82.1 %copy-start.7 = (f32[64,256]{1,0:T(8,128)S(1)}, f32[64,256]{1,0:T(8,128)}, u32[]{:S(2)}) copy-start(f32[64,256]{1,0:T(8,128)} %reduce-scatter.3.cloned.1.call-done) | copy-start | bytes 196612
  1261.1 183.5 %copy-start.5 = (f32[64,256]{1,0:T(8,128)S(1)}, f32[64,256]{1,0:T(8,128)}, u32[]{:S(2)}) copy-start(f32[64,256]{1,0:T(8,128)} %param.18) | copy-start | bytes 196612
  1261.1 183.5 %copy-start.6 = (f32[64,256]{1,0:T(8,128)S(1)}, f32[64,256]{1,0:T(8,128)}, u32[]{:S(2)}) copy-start(f32[64,256]{1,0:T(8,128)} %all-reduce.4.cloned.1.call-done) | copy-start | bytes 196612
Sparse Core Ops, SparseCore 0:
  10.7 126.3 all-gather.2
  374.0 92.8 all-reduce.3
  472.0 84.0 reduce-scatter.2
  558.7 121.4 all-gather.4
  748.7 510.7 all-reduce.7
  1264.4 78.6 reduce-scatter.4
  1346.6 97.8 all-reduce.5
where the time goes:
time: 1450 us
  waiting for transfers between devices  1050 us (72%)
  blocking collectives  291 us (20%)
  starting transfers between devices  41.7 us (3%)
  other arithmetic  20.8 us (1%)
    psum x1, waiting for transfers between devices, local(): context_grad = lax.psum(ctx_acc, ('blk', 'rows')) * grad_scale  516 us
    all_to_all x1, blocking collectives, local(): lax.all_to_all(item_acc.reshape(blk_count, block_edge, factor_rank), 'blk...  219 us
    psum x2, waiting for transfers between devices, local(): item_grad = lax.psum(jnp.sum(received, axis=0), 'rows')  192 us
    all_gather x2, waiting for transfers between devices, local(): lax.all_gather(item_factor.astype(jnp.bfloat16), 'blk', axis=0, tiled=True)  178 us
    reduce_scatter x2, waiting for transfers between devices, local(): lax.psum_scatter(user_acc, 'rows', scatter_dimension=0, tiled=True)  167 us
    all_gather x2, blocking collectives, local(): lax.all_gather(user_factor.astype(jnp.bfloat16), 'rows', axis=0, tiled=True)  71.5 us
    all_to_all x1, starting transfers between devices, local(): lax.all_to_all(item_acc.reshape(blk_count, block_edge, factor_rank), 'blk...  41.5 us
  transfers between devices with their start and end apart: 8, of which 7 were waited for; matrix products, arithmetic and copies ran while one was open for 1% of the time, Pallas kernels for 0%

commit v1 on v0

--- a/solution.py
+++ b/solution.py
@@ -119,7 +119,7 @@
         user_factor = user_factor - user_step * own_grad
         item_factor = item_factor - item_step * item_grad
         if is_last:
-            context_grad = lax.psum(ctx_acc, ("blk", "rows")) * grad_scale
+            context_grad = lax.psum(lax.psum(ctx_acc, "blk"), "rows") * grad_scale
     return (user_factor, item_factor, context_grad)
 
 

time: 1450 us -> 1380 us (0.952)
  waiting for transfers between devices: 1050 us -> 976 us
    psum x1, waiting for transfers between devices: 516 us -> 238 us  [local(): context_grad = lax.psum(lax.psum(ctx_acc, 'blk'), 'rows') * grad_scale]
    all_to_all x1, waiting for transfers between devices: 0.01 us -> 189 us  [local(): lax.all_to_all(item_acc.reshape(blk_count, block_edge, factor_rank), 'blk...]
  transfers between devices with their start and end apart: 8 -> 8, of which waited for: 7 -> 8; matrix products, arithmetic and copies ran while one was open for 1% -> 1% of each run, Pallas kernels for 0% -> 0%
where the time goes in v1:
time: 1380 us; the launch traced here: 1370 us
  waiting for transfers between devices  976 us (71%)
  blocking collectives  291 us (21%)
  starting transfers between devices  41.7 us (3%)
  other arithmetic  20.7 us (2%)
  between operations  14.2 us (1%)
    psum x1, waiting for transfers between devices, local(): context_grad = lax.psum(lax.psum(ctx_acc, 'blk'), 'rows') * grad_scale  238 us
    all_to_all x1, blocking collectives, local(): lax.all_to_all(item_acc.reshape(blk_count, block_edge, factor_rank), 'blk...  219 us
    psum x2, waiting for transfers between devices, local(): item_grad = lax.psum(jnp.sum(received, axis=0), 'rows')  193 us
    all_to_all x1, waiting for transfers between devices, local(): lax.all_to_all(item_acc.reshape(blk_count, block_edge, factor_rank), 'blk...  189 us
    all_gather x2, waiting for transfers between devices, local(): lax.all_gather(item_factor.astype(jnp.bfloat16), 'blk', axis=0, tiled=True)  178 us
    reduce_scatter x2, waiting for transfers between devices, local(): lax.psum_scatter(user_acc, 'rows', scatter_dimension=0, tiled=True)  176 us
    all_gather x2, blocking collectives, local(): lax.all_gather(user_factor.astype(jnp.bfloat16), 'rows', axis=0, tiled=True)  71.5 us
    all_to_all x1, starting transfers between devices, local(): lax.all_to_all(item_acc.reshape(blk_count, block_edge, factor_rank), 'blk...  41.5 us
  transfers between devices with their start and end apart: 8, of which 8 were waited for; matrix products, arithmetic and copies ran while one was open for 1% of the time, Pallas kernels for 0%

profile of v1, /device:TPU:32, one launch (start us, length us, event | category | flops | bytes accessed | tf_op | source)
XLA Modules:
  0.0 1374.0 jit_solution(11142551886250670328)
XLA Ops:
  7.2 1.5 convert_element_type.100
  8.7 0.8 convert_element_type.99
  9.6 0.9 convert_element_type.101
  10.5 35.1 %all_gather.12 = bf16[512,256]{1,0:T(8,128)(2,1)S(1)} all-gather(bf16[64,256]{1,0:T(8,128)(2,1)S(1)} %convert_element_type.99), channel_id=1, replica_groups=mesh['blk'=64,'rows'=8] {'rows'}, dimensions={0}, use_global_device_ids=true | all-gather | bytes 294912 | tf_op jit(solution)/shard_map/all_gather | solution.py:79
  45.6 91.5 %all-gather.3.cloned.1.call-done = bf16[4096,256]{1,0:T(8,128)(2,1)} async-done(((bf16[64,256]{1,0:T(8,128)(2,1)}), bf16[4096,256]{1,0:T(8,128)(2,1)}) %all-gather.3.cloned.1.call-update) | async-done | bytes 2097168 | tf_op jit(solution)/shard_map/all_gather | solution.py:80
  137.2 2.2 broadcast.33.clone
  139.4 12.0 while.30
  140.1 0.6 dynamic_slice.119
  141.3 0.6 dynamic_slice.121
  142.5 0.6 dynamic_slice.120
  143.8 0.8 dynamic-slice_convert_fusion.10
  144.6 0.7 multiply_convert_fusion.24
  145.3 1.8 fusion.57
  147.6 1.1 reshape.90
  148.7 2.0 fusion.59
  151.4 219.3 %all_to_all.10 = f32[64,64,256]{2,1,0:T(8,128)} all-to-all(f32[64,64,256]{2,1,0:T(8,128)} %bitcast.101), channel_id=1, replica_groups=mesh['blk'=64,'rows'=8] {'blk'}, dimensions={0} | all-to-all | bytes 8388608 | tf_op jit(solution)/shard_map/all_to_all | solution.py:111
  370.7 3.1 reduce_sum.18
  373.9 0.7 reduce-scatter.3.cloned.1.call-update
  374.6 92.3 %all-reduce.5.cloned.1.call-done = f32[64,256]{1,0:T(8,128)} async-done(((f32[64,256]{1,0:T(8,128)}), f32[64,256]{1,0:T(8,128)}) %all-reduce.5.cloned.1.call-update) | async-done | bytes 65552 | tf_op jit(solution)/shard_map/psum | solution.py:118
  466.9 1.5 fusion.24
  468.4 87.7 %reduce-scatter.3.cloned.1.call-done = f32[64,256]{1,0:T(8,128)} async-done(((f32[512,256]{1,0:T(8,128)}), f32[64,256]{1,0:T(8,128)}) %reduce-scatter.3.cloned.1.call-update) | async-done | bytes 65552 | tf_op jit(solution)/shard_map/reduce_scatter | solution.py:110
  556.1 0.9 fusion.23
  557.0 36.4 %all_gather.14 = bf16[512,256]{1,0:T(8,128)(2,1)} all-gather(bf16[64,256]{1,0:T(8,128)(2,1)S(1)} %fusion.23), channel_id=1, replica_groups=mesh['blk'=64,'rows'=8] {'rows'}, dimensions={0}, use_global_device_ids=true | all-gather | bytes 294912 | tf_op jit(solution)/shard_map/all_gather | solution.py:79
  593.4 86.8 %all-gather.5.cloned.1.call-done = bf16[4096,256]{1,0:T(8,128)(2,1)} async-done(((bf16[64,256]{1,0:T(8,128)(2,1)}), bf16[4096,256]{1,0:T(8,128)(2,1)}) %all-gather.5.cloned.1.call-update) | async-done | bytes 2097168 | tf_op jit(solution)/shard_map/all_gather | solution.py:80
  680.2 2.3 broadcast.33
  682.5 17.4 %while.31 = (s32[]{:T(128)}, f32[512,256]{1,0:T(8,128)S(1)}, f32[4096,256]{1,0:T(8,128)}, f32[128,256]{1,0:T(8,128)S(1)}, s32[]{:T(128)}, /*index=5*/s32[3]{0:T(...) while((s32[]{:T(128)}, f32[512,256]{1,0:T(8,128)S(1)}, ...), condition=%wide.region_6.7_spmd, body=%wide.region_5.6_spmd.sunk | while | flops 544047104 | bytes 16253349 | solution.py:107
  683.1 0.6 dynamic_slice.129
  684.4 0.6 dynamic_slice.131
  685.6 0.6 dynamic_slice.130
  686.9 0.8 dynamic-slice_convert_fusion.13
  687.6 0.8 dynamic-slice_convert_fusion.12
  688.4 1.5 multiply_convert_fusion.26
  689.9 1.8 fusion.67
  692.2 2.1 reshape.92
  694.3 1.8 fusion.70
  696.0 1.1 reshape.91
  697.2 2.0 fusion.69
  699.9 0.8 copy-done
  700.7 41.5 %all-to-all-start.1 = ((f32[64,64,256]{2,1,0:T(8,128)}), f32[64,64,256]{2,1,0:T(8,128)}, u32[]{:S(2)}, u32[]{:S(2)}) async-start(f32[64,64,256]{2,1,0:T(8,128)} %bitcast.100), calls=%async_computation.3 | async-start | bytes 8388608 | tf_op jit(solution)/shard_map/all_to_all | solution.py:111
  742.2 0.5 all-reduce.7.cloned.1.call-update
  743.4 188.6 %all-to-all-done.1 = f32[64,64,256]{2,1,0:T(8,128)} async-done(((f32[64,64,256]{2,1,0:T(8,128)}), f32[64,64,256]{2,1,0:T(8,128)}, u32[]{:S(2)}, u32[]{:S(2)}) %all-to-all-start.1) | async-done | bytes 4194336 | tf_op jit(solution)/shard_map/all_to_all | solution.py:111
  932.1 3.1 reduce_sum.19
  935.1 238.3 %all-reduce.7.cloned.1.call-done = f32[128,256]{1,0:T(8,128)} async-done(((f32[128,256]{1,0:T(8,128)}), f32[128,256]{1,0:T(8,128)}) %all-reduce.7.cloned.1.call-update) | async-done | bytes 131088 | tf_op jit(solution)/shard_map/psum | solution.py:122
  1173.5 88.1 %reduce-scatter.5.cloned.1.call-done = f32[64,256]{1,0:T(8,128)} async-done(((f32[512,256]{1,0:T(8,128)}), f32[64,256]{1,0:T(8,128)}) %reduce-scatter.5.cloned.1.call-update) | async-done | bytes 65552 | tf_op jit(solution)/shard_map/reduce_scatter | solution.py:110
  1261.6 1.5 multiply_subtract_fusion.1
  1263.1 101.0 %all-reduce.9.cloned.1.call-done = (f32[64,256]{1,0:T(8,128)}, f32[128,256]{1,0:T(8,128)}) async-done(((f32[64,256]{1,0:T(8,128)}, f32[128,256]{1,0:T(8,128)}), (f32[64,256]{1,0:T(8,128)}, f32[128,256]{1,0:T(8,128)})) %all-reduce.9.cloned.1.call-update) | async-done | bytes 196624 | tf_op jit(solution)/shard_map/psum | solution.py:118
  1364.1 1.6 broadcast_multiply_fusion
  1365.7 1.5 multiply_subtract_fusion
  (39 shorter events, 2.0 us)
Async XLA Ops:
  7.2 129.9 %all-gather.3.cloned.1.call-start = ((), (), s32[]{:S(2)}) async-start(), calls=%async_computation.4 | async-start | bytes 2129920 | tf_op jit(solution)/shard_map/all_gather | solution.py:80
  8.7 458.2 %all-reduce.5.cloned.1.call-start = ((), (), s32[]{:S(2)}) async-start(), calls=%async_computation.6 | async-start | bytes 131072 | tf_op jit(solution)/shard_map/psum | solution.py:118
  137.1 2.3 copy-start.8
  137.1 2.3 copy-start.9
  137.1 2.2 copy-start.10
  151.4 219.3 %copy-start.1 = (f32[512,256]{1,0:T(8,128)}, f32[512,256]{1,0:T(8,128)S(1)}, u32[]{:S(2)}) copy-start(f32[512,256]{1,0:T(8,128)S(1)} %get-tuple-element.185) | copy-start | bytes 1572868
  370.7 96.2 %copy-start.4 = (f32[64,256]{1,0:T(8,128)S(1)}, f32[64,256]{1,0:T(8,128)}, u32[]{:S(2)}) copy-start(f32[64,256]{1,0:T(8,128)} %param.18) | copy-start | bytes 196612
  370.7 185.4 %copy-start.3 = (f32[64,256]{1,0:T(8,128)S(1)}, f32[64,256]{1,0:T(8,128)}, u32[]{:S(2)}) copy-start(f32[64,256]{1,0:T(8,128)} %param.17) | copy-start | bytes 196612
  373.8 182.3 %reduce-scatter.3.cloned.1.call-start = ((), (), s32[]{:S(2)}) async-start(), calls=%async_computation.5 | async-start | bytes 589824 | tf_op jit(solution)/shard_map/reduce_scatter | solution.py:110
  374.6 305.6 %all-gather.5.cloned.1.call-start = ((), (), s32[]{:S(2)}) async-start(), calls=%async_computation.7 | async-start | bytes 2129920 | tf_op jit(solution)/shard_map/all_gather | solution.py:80
  699.9 0.9 copy-start
  699.9 0.9 copy-start.2
  700.7 231.4 %all-to-all-start.1 = ((f32[64,64,256]{2,1,0:T(8,128)}), f32[64,64,256]{2,1,0:T(8,128)}, u32[]{:S(2)}, u32[]{:S(2)}) async-start(f32[64,64,256]{2,1,0:T(8,128)} %bitcast.100), calls=%async_computation.3 | async-start | bytes 8388608 | tf_op jit(solution)/shard_map/all_to_all | solution.py:111
  742.2 431.3 %all-reduce.7.cloned.1.call-start = ((), (), s32[]{:S(2)}) async-start(), calls=%async_computation.9 | async-start | bytes 262144 | tf_op jit(solution)/shard_map/psum | solution.py:122
  742.8 518.9 %reduce-scatter.5.cloned.1.call-start = ((), (), s32[]{:S(2)}) async-start(), calls=%async_computation.8 | async-start | bytes 589824 | tf_op jit(solution)/shard_map/reduce_scatter | solution.py:110
  743.4 518.3 %copy-start.7 = (f32[64,256]{1,0:T(8,128)S(1)}, f32[64,256]{1,0:T(8,128)}, u32[]{:S(2)}) copy-start(f32[64,256]{1,0:T(8,128)} %reduce-scatter.3.cloned.1.call-done) | copy-start | bytes 196612
  743.4 622.3 %copy-start.5 = (f32[64,256]{1,0:T(8,128)S(1)}, f32[64,256]{1,0:T(8,128)}, u32[]{:S(2)}) copy-start(f32[64,256]{1,0:T(8,128)} %param.18) | copy-start | bytes 196612
  743.4 622.3 %copy-start.6 = (f32[64,256]{1,0:T(8,128)S(1)}, f32[64,256]{1,0:T(8,128)}, u32[]{:S(2)}) copy-start(f32[64,256]{1,0:T(8,128)} %all-reduce.5.cloned.1.call-done) | copy-start | bytes 196612
  743.4 620.7 %all-reduce.9.cloned.1.call-start = ((), (), s32[]{:S(2)}) async-start(), calls=%async_computation.10 | async-start | bytes 393216 | tf_op jit(solution)/shard_map/psum | solution.py:118
Sparse Core Ops, SparseCore 0:
  10.7 126.3 all-gather.2
  374.0 92.8 all-reduce.4
  472.0 84.0 reduce-scatter.2
  558.7 121.4 all-gather.4
  746.2 427.2 all-reduce.6
  1178.4 83.1 reduce-scatter.4
  1265.2 98.8 all-reduce.8
